TPU v7x, 128 devices: a whole 4x4x4 slice. The times are simulated.
128 devices in a mesh: ctx: 32 (over y, x, core), head: 4 (over z).
Axes of the slice: x: 4, y: 4, z: 4, core: 2. Of those that a mesh axis runs over, the one named last changes fastest.
Arguments:
- queries: bfloat16 [16384, 4096], P('ctx', 'head'), may hold values from -5 to 5
- keys: bfloat16 [16384, 512], P('ctx', 'head'), may hold values from -5 to 5
- values: bfloat16 [16384, 512], P('ctx', 'head'), may hold values from -6 to 6
- doc_ids: int32 [16384], replicated, may hold values from 0 to 31, never falling along the last dimension, each value on 1 to 1536 neighbouring positions
- out_weight: bfloat16 [4096, 8192], P(None, 'head'), may hold values from -0.09375 to 0.09375
Outputs:
- layer_out: bfloat16 [16384, 8192], P('ctx', 'head')
Inputs may be any that keep to these rules, and one draw needn't show every extreme that they name: `doc_ids`: every document holds at most 1536 tokens, and one holds exactly that many.
All inputs are finite; a program needn't handle non-finite values.
Results may differ from a plain program's by a relative error of at most 0.0053.
Values may be sent and summed in bfloat16 or wider, within the bound.
No kernel may reach another device: no remote copies, remote signals or barrier semaphores. Data moves between devices by JAX's collectives and lax.ppermute only.
A program may use at most 128 MiB of HBM per device.

v0:
```python
import jax
import jax.numpy as jnp
from jax import lax
from jax.sharding import PartitionSpec as P

HEAD_SIZE = 128
REACH = 3


def from_behind(block, axis, distance):
    devices = range(lax.axis_size(axis))
    route = [(i - distance, i) for i in devices if i - distance in devices]
    return lax.ppermute(block, axis, route)


def attend_window(queries, key_all, value_all, visible):
    rows_here = queries.shape[0]
    kv_heads = key_all.shape[1] // HEAD_SIZE
    group_width = queries.shape[1] // key_all.shape[1]
    local_span = key_all.shape[0]
    query_heads = queries.reshape(rows_here, kv_heads, group_width, HEAD_SIZE)
    key_heads = key_all.reshape(local_span, kv_heads, HEAD_SIZE)
    value_heads = value_all.reshape(local_span, kv_heads, HEAD_SIZE)
    scores = jnp.einsum(
        "qgjd,kgd->gjqk", query_heads, key_heads, preferred_element_type=jnp.float32
    ) * HEAD_SIZE ** (-0.5)
    masked = jnp.where(visible, scores, -jnp.inf)
    row_peak = jnp.max(masked, axis=3, keepdims=True)
    exponent = jnp.where(visible, jnp.exp(scores - row_peak), 0.0)
    row_total = jnp.sum(exponent, axis=3, keepdims=True)
    weights = exponent.astype(jnp.bfloat16)
    mixture = (
        jnp.einsum("gjqk,kgd->gjqd", weights, value_heads, preferred_element_type=jnp.float32)
        / row_total
    )
    return (
        jnp.transpose(mixture, (2, 0, 1, 3))
        .reshape(rows_here, queries.shape[1])
        .astype(jnp.bfloat16)
    )


def shards(queries, keys, values, doc_ids, out_weight):
    rows_here = keys.shape[0]
    shard_index = lax.axis_index("ctx")
    key_parts = []
    value_parts = []
    for offset in range(REACH, 0, -1):
        arrived = from_behind((keys, values), "ctx", offset)
        key_parts.append(arrived[0])
        value_parts.append(arrived[1])
    key_all = jnp.concatenate(key_parts + [keys], 0)
    value_all = jnp.concatenate(value_parts + [values], 0)
    local_span = key_all.shape[0]
    leading_rows = REACH * rows_here
    doc_pad = jnp.concatenate([jnp.full((leading_rows,), -1, jnp.int32), doc_ids], 0)
    first_row = shard_index * rows_here
    key_docs = lax.dynamic_slice_in_dim(doc_pad, first_row, local_span, 0)
    query_docs = lax.dynamic_slice_in_dim(doc_ids, first_row, rows_here, 0)
    key_rel = lax.iota(jnp.int32, local_span)
    query_rel = leading_rows + lax.iota(jnp.int32, rows_here)
    visible = (query_docs[:, None] == key_docs[None, :]) & (key_rel[None, :] <= query_rel[:, None])
    attended = attend_window(queries, key_all, value_all, visible)
    projected = jnp.dot(
        lax.all_gather(attended, "head", axis=1, tiled=True),
        out_weight,
        preferred_element_type=jnp.float32,
    )
    return projected.astype(jnp.bfloat16)


def solution(mesh):
    in_specs = (P("ctx", "head"), P("ctx", "head"), P("ctx", "head"), P(), P(None, "head"))
    out_specs = P("ctx", "head")
    return jax.shard_map(shards, mesh=mesh, in_specs=in_specs, out_specs=out_specs, check_vma=False)
```

profile of v0, /device:TPU:1, one launch (start us, length us, event | category | flops | bytes accessed | tf_op | source)
XLA Modules:
  0.0 145.0 jit_solution(6102187642814633350)
XLA Ops:
  6.5 0.0 copy-start
  6.5 0.0 all-gather.2.cloned.1.call-start
  6.5 1.1 copy.7
  7.6 4.5 %collective-permute-start.5 = (bf16[512,128]{0,1:T(8,128)(2,1)S(1)}, bf16[512,128]{0,1:T(8,128)(2,1)S(1)}, u32[]{:S(2)}, u32[]{:S(2)}) collective-permute-start(bf16[512,128]{0,1:T(8,128)(2,1)S(1)} %copy.7), channel_id=1, source_target_pairs={{0,4},{4,8},{8,12},{12,16},{16,20},{20,24},{24,28},{28,32},{32,36}... | collective-permute-start | bytes 393224 | tf_op jit(solution)/shard_map/ppermute | solution.py:13
  12.2 3.1 %collective-permute-start.4 = (bf16[512,128]{0,1:T(8,128)(2,1)S(1)}, bf16[512,128]{0,1:T(8,128)(2,1)S(1)}, u32[]{:S(2)}, u32[]{:S(2)}) collective-permute-start(bf16[512,128]{0,1:T(8,128)(2,1)S(1)} %copy.7), channel_id=1, source_target_pairs={{0,8},{4,12},{8,16},{12,20},{16,24},{20,28},{24,32},{28,36},{32,40... | collective-permute-start | bytes 393224 | tf_op jit(solution)/shard_map/ppermute | solution.py:13
  15.3 2.8 %collective-permute-start.1 = (bf16[512,128]{1,0:T(8,128)(2,1)}, bf16[512,128]{1,0:T(8,128)(2,1)S(1)}, u32[]{:S(2)}, u32[]{:S(2)}) collective-permute-start(bf16[512,128]{1,0:T(8,128)(2,1)} %param.6), channel_id=1, source_target_pairs={{0,8},{4,12},{8,16},{12,20},{16,24},{20,28},{24,32},{28,36},{32,40... | collective-permute-start | bytes 393224 | tf_op jit(solution)/shard_map/ppermute | solution.py:13
  18.1 4.0 %collective-permute-start = (bf16[512,128]{1,0:T(8,128)(2,1)}, bf16[512,128]{1,0:T(8,128)(2,1)S(1)}, u32[]{:S(2)}, u32[]{:S(2)}) collective-permute-start(bf16[512,128]{1,0:T(8,128)(2,1)} %param.6), channel_id=1, source_target_pairs={{0,12},{4,16},{8,20},{12,24},{16,28},{20,32},{24,36},{28,40},{32,4... | collective-permute-start | bytes 393224 | tf_op jit(solution)/shard_map/ppermute | solution.py:13
  22.1 2.5 %collective-permute-start.2 = (bf16[512,128]{1,0:T(8,128)(2,1)}, bf16[512,128]{1,0:T(8,128)(2,1)S(1)}, u32[]{:S(2)}, u32[]{:S(2)}) collective-permute-start(bf16[512,128]{1,0:T(8,128)(2,1)} %param.6), channel_id=1, source_target_pairs={{0,4},{4,8},{8,12},{12,16},{16,20},{20,24},{24,28},{28,32},{32,36}... | collective-permute-start | bytes 393224 | tf_op jit(solution)/shard_map/ppermute | solution.py:13
  24.7 0.8 dynamic_slice.6
  25.4 0.8 pad_dynamic-slice_fusion
  26.2 0.9 fusion.9
  27.2 0.0 collective-permute-done.1
  27.2 3.5 %collective-permute-start.3 = (bf16[512,128]{0,1:T(8,128)(2,1)S(1)}, bf16[512,128]{0,1:T(8,128)(2,1)S(1)}, u32[]{:S(2)}, u32[]{:S(2)}) collective-permute-start(bf16[512,128]{0,1:T(8,128)(2,1)S(1)} %copy.7), channel_id=1, source_target_pairs={{0,12},{4,16},{8,20},{12,24},{16,28},{20,32},{24,36},{28,40},{32,4... | collective-permute-start | bytes 393224 | tf_op jit(solution)/shard_map/ppermute | solution.py:13
  30.7 0.0 collective-permute-done
  30.7 0.0 collective-permute-done.2
  30.7 14.3 %fusion = (f32[8,512]{1,0:T(8,128)S(1)}, f32[2048,512,8]{1,0,2:T(8,128)}) fusion(pred[512,2048]{0,1:T(8,128)(4,1)S(1)} %fusion.9, bf16[512,128]{1,0:T(8,128)(2,1)} %param.6, bf16[512,128]{1,0:T(8,128)(2,1)S(1)} %collective-permute-done.2, bf16[512,128]{1,0:T(8,128)(2,1)S(1)} %collective-permute-done.1, bf16[512,128]{1,0:T(8,128)(2,1)S(1)} %collective-permute-done, ...), kind=kOutput, calls=%fused_computation.2 | convolution fusion | flops 2174742528 | bytes 36192256 | tf_op jit(solution)/shard_map/qgjd,kgd->gjqk/dot_general | solution.py:24
  45.0 14.4 %fusion.3 = f32[8,512]{1,0:T(8,128)S(1)} fusion(f32[2048,512,8]{1,0,2:T(8,128)} %get-tuple-element.6, f32[8,512]{1,0:T(8,128)S(1)} %get-tuple-element.5, pred[512,2048]{0,1:T(8,128)(4,1)S(1)} %fusion.9), kind=kLoop, calls=%fused_computation.5 | loop fusion | flops 33550336 | bytes 34635776 | tf_op jit(solution)/shard_map/reduce_sum | solution.py:30
  59.4 0.0 collective-permute-done.5
  59.4 0.0 collective-permute-done.4
  59.4 0.0 collective-permute-done.3
  59.4 15.5 %divide_convert_fusion = bf16[8,512,128]{1,2,0:T(8,128)(2,1)} fusion(f32[8,512]{1,0:T(8,128)S(1)} %fusion.3, f32[2048,512,8]{1,0,2:T(8,128)} %get-tuple-element.6, f32[8,512]{1,0:T(8,128)S(1)} %get-tuple-element.5, pred[512,2048]{0,1:T(8,128)(4,1)S(1)} %fusion.9, bf16[512,128]{0,1:T(8,128)(2,1)S(1)} %copy.7, ...), kind=kOutput, calls=%fused_computation.13 | convolution fusion | flops 2184183808 | bytes 36208640 | tf_op jit(solution)/shard_map/gjqk,kgd->gjqd/dot_general | solution.py:33
  74.9 0.0 all-gather.2.cloned.1.call-update
  75.0 48.6 %all-gather.2.cloned.1.call-done = bf16[512,4096]{0,1:T(8,128)(2,1)} async-done(((bf16[512,1024]{0,1:T(8,128)(2,1)}), bf16[512,4096]{0,1:T(8,128)(2,1)}) %all-gather.2.cloned.1.call-update) | async-done | bytes 4194320 | tf_op jit(solution)/shard_map/all_gather | solution.py:65
  123.6 14.6 %convolution_convert_fusion = bf16[512,2048]{1,0:T(8,128)(2,1)} fusion(bf16[512,4096]{0,1:T(8,128)(2,1)} %all-gather.2.cloned.1.call-done, bf16[4096,2048]{1,0:T(8,128)(2,1)} %param.9), kind=kOutput, calls=%fused_computation.12 | convolution fusion | flops 8590983168 | bytes 23068672 | tf_op jit(solution)/shard_map/dot_general | solution.py:64
  (2 shorter events, 0.0 us)
Async XLA Ops:
  6.5 24.1 %copy-start = (bf16[512,1024]{1,0:T(8,128)(2,1)S(1)}, bf16[512,1024]{1,0:T(8,128)(2,1)}, u32[]{:S(2)}) copy-start(bf16[512,1024]{1,0:T(8,128)(2,1)} %param.5) | copy-start | bytes 3145732
  6.5 117.1 %all-gather.2.cloned.1.call-start = ((), (), s32[]{:S(2)}) async-start(), calls=%async_computation | async-start | bytes 5242880 | tf_op jit(solution)/shard_map/all_gather | solution.py:65
  7.6 51.8 %collective-permute-start.5 = (bf16[512,128]{0,1:T(8,128)(2,1)S(1)}, bf16[512,128]{0,1:T(8,128)(2,1)S(1)}, u32[]{:S(2)}, u32[]{:S(2)}) collective-permute-start(bf16[512,128]{0,1:T(8,128)(2,1)S(1)} %copy.7), channel_id=1, source_target_pairs={{0,4},{4,8},{8,12},{12,16},{16,20},{20,24},{24,28},{28,32},{32,36}... | collective-permute-start | bytes 393224 | tf_op jit(solution)/shard_map/ppermute | solution.py:13
  12.2 47.3 %collective-permute-start.4 = (bf16[512,128]{0,1:T(8,128)(2,1)S(1)}, bf16[512,128]{0,1:T(8,128)(2,1)S(1)}, u32[]{:S(2)}, u32[]{:S(2)}) collective-permute-start(bf16[512,128]{0,1:T(8,128)(2,1)S(1)} %copy.7), channel_id=1, source_target_pairs={{0,8},{4,12},{8,16},{12,20},{16,24},{20,28},{24,32},{28,36},{32,40... | collective-permute-start | bytes 393224 | tf_op jit(solution)/shard_map/ppermute | solution.py:13
  15.3 11.9 %collective-permute-start.1 = (bf16[512,128]{1,0:T(8,128)(2,1)}, bf16[512,128]{1,0:T(8,128)(2,1)S(1)}, u32[]{:S(2)}, u32[]{:S(2)}) collective-permute-start(bf16[512,128]{1,0:T(8,128)(2,1)} %param.6), channel_id=1, source_target_pairs={{0,8},{4,12},{8,16},{12,20},{16,24},{20,28},{24,32},{28,36},{32,40... | collective-permute-start | bytes 393224 | tf_op jit(solution)/shard_map/ppermute | solution.py:13
  18.1 12.5 %collective-permute-start = (bf16[512,128]{1,0:T(8,128)(2,1)}, bf16[512,128]{1,0:T(8,128)(2,1)S(1)}, u32[]{:S(2)}, u32[]{:S(2)}) collective-permute-start(bf16[512,128]{1,0:T(8,128)(2,1)} %param.6), channel_id=1, source_target_pairs={{0,12},{4,16},{8,20},{12,24},{16,28},{20,32},{24,36},{28,40},{32,4... | collective-permute-start | bytes 393224 | tf_op jit(solution)/shard_map/ppermute | solution.py:13
  22.1 8.5 %collective-permute-start.2 = (bf16[512,128]{1,0:T(8,128)(2,1)}, bf16[512,128]{1,0:T(8,128)(2,1)S(1)}, u32[]{:S(2)}, u32[]{:S(2)}) collective-permute-start(bf16[512,128]{1,0:T(8,128)(2,1)} %param.6), channel_id=1, source_target_pairs={{0,4},{4,8},{8,12},{12,16},{16,20},{20,24},{24,28},{28,32},{32,36}... | collective-permute-start | bytes 393224 | tf_op jit(solution)/shard_map/ppermute | solution.py:13
  27.2 32.3 %collective-permute-start.3 = (bf16[512,128]{0,1:T(8,128)(2,1)S(1)}, bf16[512,128]{0,1:T(8,128)(2,1)S(1)}, u32[]{:S(2)}, u32[]{:S(2)}) collective-permute-start(bf16[512,128]{0,1:T(8,128)(2,1)S(1)} %copy.7), channel_id=1, source_target_pairs={{0,12},{4,16},{8,20},{12,24},{16,28},{20,32},{24,36},{28,40},{32,4... | collective-permute-start | bytes 393224 | tf_op jit(solution)/shard_map/ppermute | solution.py:13
Sparse Core Ops, SparseCore 0:
  75.1 48.4 all-gather.1
where the time goes:
time: 145 us
  waiting for transfers between devices  48.7 us (34%)
  matrix products  44.4 us (31%)
  starting transfers between devices  20.4 us (14%)
  other arithmetic  15.3 us (11%)
  between operations  13.5 us (9%)
  local copies, waits for them, and re-layouts  2.64 us (2%)
    all_gather x1, waiting for transfers between devices, shards(): lax.all_gather(attended, 'head', axis=1, tiled=True)  48.6 us
    ppermute x6, starting transfers between devices, from_behind(): return lax.ppermute(block, axis, route)  20.4 us
    dot_general x1, matrix products, attend_window(): jnp.einsum('gjqk,kgd->gjqd', weights, value_heads, preferred_element_type...  15.5 us
    dot_general x1, matrix products, shards(): jnp.dot(lax.all_gather(attended, 'head', axis=1, tiled=True), out_weight,...  14.6 us
    reduce_sum x1, other arithmetic, attend_window(): row_total = jnp.sum(exponent, axis=3, keepdims=True)  14.4 us
    dot_general x1, matrix products, attend_window(): jnp.einsum('qgjd,kgd->gjqk', query_heads, key_heads, preferred_element_ty...  14.3 us
  transfers between devices with their start and end apart: 7, of which 1 were waited for; matrix products, arithmetic and copies ran while one was open for 22% of the time, Pallas kernels for 0%

commit v1 on v0

--- a/solution.py
+++ b/solution.py
@@ -1,3 +1,4 @@
+import functools
 import jax
 import jax.numpy as jnp
 from jax import lax
@@ -5,6 +6,35 @@
 
 HEAD_SIZE = 128
 REACH = 3
+
+
+def track_ends(body, axis_id, dim_no):
+    then = lax.axis_size(axis_id)
+    wide_out, current_value, placed = (then, lax.axis_index(axis_id), body.shape[dim_no])
+    earlier = range(wide_out)
+    raw_out = map(lambda idx: (idx, (idx + 1) % wide_out), earlier)
+    ledger = list(map(lambda idx: (idx, (idx - 1) % wide_out), range(wide_out)))
+    carry_in = jnp.zeros(
+        (*body.shape[:dim_no], wide_out * placed, *body.shape[dim_no + 1 :]), body.dtype
+    )
+    windows = list(raw_out)
+    z1 = piece_now = body
+    carry_in = lax.dynamic_update_slice_in_dim(carry_in, body, current_value * placed, axis=dim_no)
+    low = wide_out // 2
+    for num in tuple(range(1, low + 1)):
+        z1 = lax.ppermute(z1, axis_id, windows)
+        carry_in = lax.dynamic_update_slice_in_dim(
+            carry_in, z1, (current_value - num) % wide_out * placed, axis=dim_no
+        )
+        if num < wide_out - low:
+            piece_now = lax.ppermute(piece_now, axis_id, ledger)
+            carry_in = lax.dynamic_update_slice_in_dim(
+                carry_in, piece_now, (current_value + num) % wide_out * placed, axis=dim_no
+            )
+    return carry_in
+
+
+measure_tokens = functools.partial(track_ends, axis_id="head", dim_no=1)
 
 
 def from_behind(block, axis, distance):
@@ -61,11 +91,7 @@
     query_rel = leading_rows + lax.iota(jnp.int32, rows_here)
     visible = (query_docs[:, None] == key_docs[None, :]) & (key_rel[None, :] <= query_rel[:, None])
     attended = attend_window(queries, key_all, value_all, visible)
-    projected = jnp.dot(
-        lax.all_gather(attended, "head", axis=1, tiled=True),
-        out_weight,
-        preferred_element_type=jnp.float32,
-    )
+    projected = jnp.dot(measure_tokens(attended), out_weight, preferred_element_type=jnp.float32)
     return projected.astype(jnp.bfloat16)
 
 

time: 145 us -> 136 us (0.938)
  between operations: 13.5 us -> 0.19 us
  starting transfers between devices: 20.4 us -> 24.7 us
  local copies, waits for them, and re-layouts: 2.64 us -> 5.71 us
  waiting for transfers between devices: 48.7 us -> 46.9 us
  matrix products: 44.4 us -> 42.6 us
    all_gather x1 -> x0, waiting for transfers between devices: 48.6 us -> none  [shards(): lax.all_gather(attended, 'head', axis=1, tiled=True)]
    ppermute x0 -> x3, waiting for transfers between devices: none -> 46.9 us  [the longest x2 46.9 us: track_ends(): z1 = lax.ppermute(z1, axis_id, windows)]
    ppermute x0 -> x3, starting transfers between devices: none -> 3.92 us  [the longest x1 2.2 us: track_ends(): piece_now = lax.ppermute(piece_now, axis_id, ledger)]
    dynamic_update_slice x0 -> x4, local copies, waits for them, and re-layouts: none -> 2.87 us  [the longest x2 1.43 us: track_ends(): lax.dynamic_update_slice_in_dim(carry_in, z1, (current_value - num) % wid...]
  transfers between devices with their start and end apart: 7 -> 9, of which waited for: 1 -> 2; matrix products, arithmetic and copies ran while one was open for 22% -> 25% of each run, Pallas kernels for 0% -> 0%
where the time goes in v1:
time: 136 us; the launch traced here: 135 us
  waiting for transfers between devices  46.9 us (34%)
  matrix products  42.6 us (31%)
  starting transfers between devices  24.7 us (18%)
  other arithmetic  15.3 us (11%)
  local copies, waits for them, and re-layouts  5.71 us (4%)
    ppermute x2, waiting for transfers between devices, track_ends(): z1 = lax.ppermute(z1, axis_id, windows)  46.9 us
    ppermute x6, starting transfers between devices, from_behind(): return lax.ppermute(block, axis, route)  20.8 us
    dot_general x1, matrix products, attend_window(): jnp.einsum('gjqk,kgd->gjqd', weights, value_heads, preferred_element_type...  14.5 us
    reduce_sum x1, other arithmetic, attend_window(): row_total = jnp.sum(exponent, axis=3, keepdims=True)  14.4 us
    dot_general x1, matrix products, attend_window(): jnp.einsum('qgjd,kgd->gjqk', query_heads, key_heads, preferred_element_ty...  14.3 us
    dot_general x1, matrix products, shards(): jnp.dot(measure_tokens(attended), out_weight, preferred_element_type=jnp....  13.7 us
  transfers between devices with their start and end apart: 9, of which 2 were waited for; matrix products, arithmetic and copies ran while one was open for 25% of the time, Pallas kernels for 0%

profile of v1, /device:TPU:1, one launch (start us, length us, event | category | flops | bytes accessed | tf_op | source)
XLA Modules:
  0.0 135.5 jit_solution(9290688750060057690)
XLA Ops:
  0.0 6.2 %collective-permute-start = (bf16[512,128]{1,0:T(8,128)(2,1)}, bf16[512,128]{1,0:T(8,128)(2,1)S(1)}, u32[]{:S(2)}, u32[]{:S(2)}) collective-permute-start(bf16[512,128]{1,0:T(8,128)(2,1)} %param.6), channel_id=1, source_target_pairs={{0,12},{4,16},{8,20},{12,24},{16,28},{20,32},{24,36},{28,40},{32,4... | collective-permute-start | bytes 393224 | tf_op jit(solution)/shard_map/ppermute | solution.py:43
  6.2 2.2 %collective-permute-start.1 = (bf16[512,128]{1,0:T(8,128)(2,1)}, bf16[512,128]{1,0:T(8,128)(2,1)S(1)}, u32[]{:S(2)}, u32[]{:S(2)}) collective-permute-start(bf16[512,128]{1,0:T(8,128)(2,1)} %param.6), channel_id=1, source_target_pairs={{0,8},{4,12},{8,16},{12,20},{16,24},{20,28},{24,32},{28,36},{32,40... | collective-permute-start | bytes 393224 | tf_op jit(solution)/shard_map/ppermute | solution.py:43
  8.4 2.2 %collective-permute-start.2 = (bf16[512,128]{1,0:T(8,128)(2,1)}, bf16[512,128]{1,0:T(8,128)(2,1)S(1)}, u32[]{:S(2)}, u32[]{:S(2)}) collective-permute-start(bf16[512,128]{1,0:T(8,128)(2,1)} %param.6), channel_id=1, source_target_pairs={{0,4},{4,8},{8,12},{12,16},{16,20},{20,24},{24,28},{28,32},{32,36}... | collective-permute-start | bytes 393224 | tf_op jit(solution)/shard_map/ppermute | solution.py:43
  10.6 1.0 copy.7
  11.6 4.8 %collective-permute-start.3 = (bf16[512,128]{0,1:T(8,128)(2,1)S(1)}, bf16[512,128]{0,1:T(8,128)(2,1)S(1)}, u32[]{:S(2)}, u32[]{:S(2)}) collective-permute-start(bf16[512,128]{0,1:T(8,128)(2,1)S(1)} %copy.7), channel_id=1, source_target_pairs={{0,12},{4,16},{8,20},{12,24},{16,28},{20,32},{24,36},{28,40},{32,4... | collective-permute-start | bytes 393224 | tf_op jit(solution)/shard_map/ppermute | solution.py:43
  16.4 3.1 %collective-permute-start.4 = (bf16[512,128]{0,1:T(8,128)(2,1)S(1)}, bf16[512,128]{0,1:T(8,128)(2,1)S(1)}, u32[]{:S(2)}, u32[]{:S(2)}) collective-permute-start(bf16[512,128]{0,1:T(8,128)(2,1)S(1)} %copy.7), channel_id=1, source_target_pairs={{0,8},{4,12},{8,16},{12,20},{16,24},{20,28},{24,32},{28,36},{32,40... | collective-permute-start | bytes 393224 | tf_op jit(solution)/shard_map/ppermute | solution.py:43
  19.5 0.8 pad_dynamic-slice_fusion
  20.3 0.8 dynamic_slice.6
  21.1 0.9 fusion.9
  22.1 2.4 %collective-permute-start.5 = (bf16[512,128]{0,1:T(8,128)(2,1)S(1)}, bf16[512,128]{0,1:T(8,128)(2,1)S(1)}, u32[]{:S(2)}, u32[]{:S(2)}) collective-permute-start(bf16[512,128]{0,1:T(8,128)(2,1)S(1)} %copy.7), channel_id=1, source_target_pairs={{0,4},{4,8},{8,12},{12,16},{16,20},{20,24},{24,28},{28,32},{32,36}... | collective-permute-start | bytes 393224 | tf_op jit(solution)/shard_map/ppermute | solution.py:43
  24.5 14.3 %fusion = (f32[8,512]{1,0:T(8,128)S(1)}, f32[2048,512,8]{1,0,2:T(8,128)}) fusion(pred[512,2048]{0,1:T(8,128)(4,1)S(1)} %fusion.9, bf16[512,128]{1,0:T(8,128)(2,1)} %param.6, bf16[512,128]{1,0:T(8,128)(2,1)S(1)} %collective-permute-done.2, bf16[512,128]{1,0:T(8,128)(2,1)S(1)} %collective-permute-done.1, bf16[512,128]{1,0:T(8,128)(2,1)S(1)} %collective-permute-done, ...), kind=kOutput, calls=%fused_computation.2 | convolution fusion | flops 2174742528 | bytes 36192256 | tf_op jit(solution)/shard_map/qgjd,kgd->gjqk/dot_general | solution.py:54
  38.8 14.4 %fusion.3 = f32[8,512]{1,0:T(8,128)S(1)} fusion(f32[2048,512,8]{1,0,2:T(8,128)} %get-tuple-element.6, f32[8,512]{1,0:T(8,128)S(1)} %get-tuple-element.5, pred[512,2048]{0,1:T(8,128)(4,1)S(1)} %fusion.9), kind=kLoop, calls=%fused_computation.5 | loop fusion | flops 33550336 | bytes 34635776 | tf_op jit(solution)/shard_map/reduce_sum | solution.py:60
  53.2 14.5 %divide_convert_fusion = bf16[8,512,128]{1,2,0:T(8,128)(2,1)S(1)} fusion(f32[8,512]{1,0:T(8,128)S(1)} %fusion.3, f32[2048,512,8]{1,0,2:T(8,128)} %get-tuple-element.6, f32[8,512]{1,0:T(8,128)S(1)} %get-tuple-element.5, pred[512,2048]{0,1:T(8,128)(4,1)S(1)} %fusion.9, bf16[512,128]{0,1:T(8,128)(2,1)S(1)} %copy.7, ...), kind=kOutput, calls=%fused_computation.13 | convolution fusion | flops 2184183808 | bytes 36208640 | tf_op jit(solution)/shard_map/gjqk,kgd->gjqd/dot_general | solution.py:63
  67.7 1.7 %collective-permute-start.6 = (bf16[512,1024]{0,1:T(8,128)(2,1)S(1)}, bf16[512,1024]{0,1:T(8,128)(2,1)S(1)}, u32[]{:S(2)}, u32[]{:S(2)}) collective-permute-start(bf16[512,1024]{0,1:T(8,128)(2,1)S(1)} %bitcast.49), channel_id=1, source_target_pairs={{0,1},{1,2},{2,3},{3,0},{4,5},{5,6},{6,7},{7,4},{8,9},{9,10},{10,1... | collective-permute-start | bytes 3145736 | tf_op jit(solution)/shard_map/ppermute | solution.py:25
  69.4 2.2 %collective-permute-start.7 = (bf16[512,1024]{0,1:T(8,128)(2,1)S(1)}, bf16[512,1024]{0,1:T(8,128)(2,1)}, u32[]{:S(2)}, u32[]{:S(2)}) collective-permute-start(bf16[512,1024]{0,1:T(8,128)(2,1)S(1)} %bitcast.50), channel_id=1, source_target_pairs={{0,3},{1,0},{2,1},{3,2},{4,7},{5,4},{6,5},{7,6},{8,11},{9,8},{10,9... | collective-permute-start | bytes 3145736 | tf_op jit(solution)/shard_map/ppermute | solution.py:30
  71.6 23.4 %collective-permute-done.6 = bf16[512,1024]{0,1:T(8,128)(2,1)S(1)} collective-permute-done((bf16[512,1024]{0,1:T(8,128)(2,1)S(1)}, bf16[512,1024]{0,1:T(8,128)(2,1)S(1)}, u32[]{:S(2)}, u32[]{:S(2)}) %collective-permute-start.6) | collective-permute-done | bytes 1048608 | tf_op jit(solution)/shard_map/ppermute | solution.py:25
  95.0 0.0 collective-permute-start.8
  95.0 0.3 broadcast_in_dim.22
  95.3 0.1 constant_dynamic-update-slice_fusion.3
  95.4 0.1 constant_dynamic-update-slice_fusion.2
  95.5 1.3 constant_dynamic-update-slice_fusion.1
  96.9 23.5 %collective-permute-done.8 = bf16[512,1024]{0,1:T(8,128)(2,1)} collective-permute-done((bf16[512,1024]{0,1:T(8,128)(2,1)S(1)}, bf16[512,1024]{0,1:T(8,128)(2,1)}, u32[]{:S(2)}, u32[]{:S(2)}) %collective-permute-start.8) | collective-permute-done | bytes 1048608 | tf_op jit(solution)/shard_map/ppermute | solution.py:25
  120.4 1.3 constant_dynamic-update-slice_fusion
  121.7 13.7 %convolution_convert_fusion = bf16[512,2048]{1,0:T(8,128)(2,1)} fusion(bf16[512,4096]{0,1:T(8,128)(2,1)S(1)} %constant_dynamic-update-slice_fusion, bf16[4096,2048]{1,0:T(8,128)(2,1)} %param.9), kind=kOutput, calls=%fused_computation.12 | convolution fusion | flops 8590983168 | bytes 23068672 | tf_op jit(solution)/shard_map/dot_general | solution.py:94
  (10 shorter events, 0.0 us)
Async XLA Ops:
  0.0 24.4 %copy-start = (bf16[512,1024]{1,0:T(8,128)(2,1)S(1)}, bf16[512,1024]{1,0:T(8,128)(2,1)}, u32[]{:S(2)}) copy-start(bf16[512,1024]{1,0:T(8,128)(2,1)} %param.5) | copy-start | bytes 3145732
  0.0 22.0 %collective-permute-start = (bf16[512,128]{1,0:T(8,128)(2,1)}, bf16[512,128]{1,0:T(8,128)(2,1)S(1)}, u32[]{:S(2)}, u32[]{:S(2)}) collective-permute-start(bf16[512,128]{1,0:T(8,128)(2,1)} %param.6), channel_id=1, source_target_pairs={{0,12},{4,16},{8,20},{12,24},{16,28},{20,32},{24,36},{28,40},{32,4... | collective-permute-start | bytes 393224 | tf_op jit(solution)/shard_map/ppermute | solution.py:43
  6.2 18.3 %collective-permute-start.1 = (bf16[512,128]{1,0:T(8,128)(2,1)}, bf16[512,128]{1,0:T(8,128)(2,1)S(1)}, u32[]{:S(2)}, u32[]{:S(2)}) collective-permute-start(bf16[512,128]{1,0:T(8,128)(2,1)} %param.6), channel_id=1, source_target_pairs={{0,8},{4,12},{8,16},{12,20},{16,24},{20,28},{24,32},{28,36},{32,40... | collective-permute-start | bytes 393224 | tf_op jit(solution)/shard_map/ppermute | solution.py:43
  8.4 16.0 %collective-permute-start.2 = (bf16[512,128]{1,0:T(8,128)(2,1)}, bf16[512,128]{1,0:T(8,128)(2,1)S(1)}, u32[]{:S(2)}, u32[]{:S(2)}) collective-permute-start(bf16[512,128]{1,0:T(8,128)(2,1)} %param.6), channel_id=1, source_target_pairs={{0,4},{4,8},{8,12},{12,16},{16,20},{20,24},{24,28},{28,32},{32,36}... | collective-permute-start | bytes 393224 | tf_op jit(solution)/shard_map/ppermute | solution.py:43
  11.6 41.5 %collective-permute-start.3 = (bf16[512,128]{0,1:T(8,128)(2,1)S(1)}, bf16[512,128]{0,1:T(8,128)(2,1)S(1)}, u32[]{:S(2)}, u32[]{:S(2)}) collective-permute-start(bf16[512,128]{0,1:T(8,128)(2,1)S(1)} %copy.7), channel_id=1, source_target_pairs={{0,12},{4,16},{8,20},{12,24},{16,28},{20,32},{24,36},{28,40},{32,4... | collective-permute-start | bytes 393224 | tf_op jit(solution)/shard_map/ppermute | solution.py:43
  16.4 36.8 %collective-permute-start.4 = (bf16[512,128]{0,1:T(8,128)(2,1)S(1)}, bf16[512,128]{0,1:T(8,128)(2,1)S(1)}, u32[]{:S(2)}, u32[]{:S(2)}) collective-permute-start(bf16[512,128]{0,1:T(8,128)(2,1)S(1)} %copy.7), channel_id=1, source_target_pairs={{0,8},{4,12},{8,16},{12,20},{16,24},{20,28},{24,32},{28,36},{32,40... | collective-permute-start | bytes 393224 | tf_op jit(solution)/shard_map/ppermute | solution.py:43
  22.1 31.1 %collective-permute-start.5 = (bf16[512,128]{0,1:T(8,128)(2,1)S(1)}, bf16[512,128]{0,1:T(8,128)(2,1)S(1)}, u32[]{:S(2)}, u32[]{:S(2)}) collective-permute-start(bf16[512,128]{0,1:T(8,128)(2,1)S(1)} %copy.7), channel_id=1, source_target_pairs={{0,4},{4,8},{8,12},{12,16},{16,20},{20,24},{24,28},{28,32},{32,36}... | collective-permute-start | bytes 393224 | tf_op jit(solution)/shard_map/ppermute | solution.py:43
  67.7 27.3 %collective-permute-start.6 = (bf16[512,1024]{0,1:T(8,128)(2,1)S(1)}, bf16[512,1024]{0,1:T(8,128)(2,1)S(1)}, u32[]{:S(2)}, u32[]{:S(2)}) collective-permute-start(bf16[512,1024]{0,1:T(8,128)(2,1)S(1)} %bitcast.49), channel_id=1, source_target_pairs={{0,1},{1,2},{2,3},{3,0},{4,5},{5,6},{6,7},{7,4},{8,9},{9,10},{10,1... | collective-permute-start | bytes 3145736 | tf_op jit(solution)/shard_map/ppermute | solution.py:25
  69.4 26.1 %collective-permute-start.7 = (bf16[512,1024]{0,1:T(8,128)(2,1)S(1)}, bf16[512,1024]{0,1:T(8,128)(2,1)}, u32[]{:S(2)}, u32[]{:S(2)}) collective-permute-start(bf16[512,1024]{0,1:T(8,128)(2,1)S(1)} %bitcast.50), channel_id=1, source_target_pairs={{0,3},{1,0},{2,1},{3,2},{4,7},{5,4},{6,5},{7,6},{8,11},{9,8},{10,9... | collective-permute-start | bytes 3145736 | tf_op jit(solution)/shard_map/ppermute | solution.py:30
  95.0 25.4 %collective-permute-start.8 = (bf16[512,1024]{0,1:T(8,128)(2,1)S(1)}, bf16[512,1024]{0,1:T(8,128)(2,1)}, u32[]{:S(2)}, u32[]{:S(2)}) collective-permute-start(bf16[512,1024]{0,1:T(8,128)(2,1)S(1)} %collective-permute-done.6), channel_id=1, source_target_pairs={{0,1},{1,2},{2,3},{3,0},{4,5},{5,6},{6,7},{7,4},{8,9},{9,10},{10,1... | collective-permute-start | bytes 3145736 | tf_op jit(solution)/shard_map/ppermute | solution.py:25
